TPU v7x, 128 devices: a whole 4x4x4 slice. The times are simulated.
128 devices in a mesh: blk: 8 (over x_hi, y), occ: 16 (over z, x_lo, core).
Axes of the slice: x: 4 (x_hi: 2, x_lo: 2; x = x_hi * 2 + x_lo), y: 4, z: 4, core: 2. Of those that a mesh axis runs over, the one named last changes fastest.
Arguments:
- tiles: bfloat16 [131072, 128], P(('blk', 'occ')), may hold values from -1.5 to 1.5
- owner: int32 [131072, 1], P(('blk', 'occ')), may hold values from 0 to 15; in each aligned block of 1024 rows (0 to 1023, 1024 to 2047, ...) at most 128 rows name the same one
- sub_block: int32 [131072], P(('blk', 'occ')), may hold values from 0 to 1
- fit_ac: bfloat16 [32, 40, 6400], P(None, None, 'occ'), may hold values from -0.29882812 to 0.29882812
- fit_bd: bfloat16 [128, 128, 6400], P('blk', None, 'occ'), may hold values from -0.29882812 to 0.29882812
Outputs:
- ladder: bfloat16 [8192, 5120], P(('blk', 'occ'))
Inputs may be any that keep to these rules, and one draw needn't show every extreme that they name: Among the 1024 tiles of one device (aligned blocks), no owner is named more than 128 times, and in every draw some owner is named exactly 128 times by some device.
All inputs are finite; a program needn't handle non-finite values.
Results may differ from a plain program's by a relative error of at most 0.005.
Values may be sent and summed in bfloat16 or wider, within the bound.
A program may use at most 192 MiB of HBM per device.

v0:
```python
import jax
import jax.numpy as jnp
from jax import lax
from jax.experimental import pallas as pl
from jax.experimental.pallas import tpu as pltpu
from jax.sharding import PartitionSpec as P

MESH = pl.DeviceIdType.MESH
RING = 4
CORES = 2
SLICES = 4
GROUPS = 2
TILES_PAIR = 16
NA, NB, NC, ND = 40, 128, 32, 128
BLOCKS_OWNER = 2
PLANE = RING * RING
A_HALF = NA // 2
PART = 640
C_PART = NC // RING
ROWS = C_PART * NA
B_CORE = 8
X_PARTS = 1
X_ROWS = ROWS // X_PARTS
K_HALF = C_PART * ND // 2
OUT_ROWS = 2 * CORES * A_HALF
B_STRIDE = 24
STEP = 256
FARTHEST_FIRST = ((10, 9, 6, 11, 8, 5, 7, 4), (14, 2, 15, 13, 1, 12, 3))

F32, BF16 = jnp.float32, jnp.bfloat16


def product(left, right, right_axis):
    return lax.dot_general(left, right, (((1,), (right_axis,)), ((), ())), preferred_element_type=F32)


def kernel(
    tiles, owner, sub_block, fit_a, fit_b, out,
    a_own, a_mate, b_own, b_mate, slots, far_out, side_out, comb_out, far_in, side_in, comb_in,
    keep_comb, keep_own, x_out, x_in, ints, summed, total, parcels, got, owners, subs, row_ids, names, final,
    load_sem, mate_s, mate_r, ring1_s, ring1_r, half1_s, half1_r, ring2_s, ring2_r, pass2_s, pass2_r,
    far_s, far_r, side_s, side_r, comb_s, comb_r, x_s, x_r, ag_s, ag_r, fw_s, fw_r, cx_s, cx_r, out_s, out_r,
):
    blk, occ = lax.axis_index("blk"), lax.axis_index("occ")
    x_hi, y = lax.div(blk, RING), lax.rem(blk, RING)
    z, x_lo, k = lax.div(occ, 4), lax.rem(lax.div(occ, 2), 2), lax.rem(occ, 2)
    x = x_hi * 2 + x_lo
    rows_dev = tiles.shape[0]
    pairs_dev = rows_dev // TILES_PAIR

    def mod(value):
        return lax.rem(value, RING)

    def device(x_at, y_at, z_at, k_at):
        return (lax.div(x_at, 2) * RING + y_at, z_at * 4 + lax.rem(x_at, 2) * 2 + k_at)

    up, down, far = mod(z + 1), mod(z + 3), mod(z + 2)
    mate = device(x, y, z, 1 - k)
    partner = device(x_hi * 2 + 1 - x_lo, y, z, k)

    def along(d):
        return device(x, y, mod(z + 1 + 2 * d), k)

    me = x * RING + y
    def cross(g, u_at, v_at):
        return (u_at, v_at) if g == 0 else (v_at, u_at)

    uv = (cross(0, x, y), cross(1, x, y))

    sizes = (PART, rows_dev + 16 - PART)

    def part_of(g, back_u, back_v, start=0, size=None):
        x_at, y_at = cross(g, mod(uv[g][0] + back_u), mod(uv[g][1] + back_v))
        return slots.at[x_at * RING + y_at, pl.ds(g * PART + start, sizes[g] if size is None else size)]

    def plane_device(g, ahead_u, ahead_v):
        return device(*cross(g, mod(uv[g][0] + ahead_u), mod(uv[g][1] + ahead_v)), z, k)

    def remote(src, dst, send, recv, to):
        return pltpu.make_async_remote_copy(
            src_ref=src, dst_ref=dst, send_sem=send, recv_sem=recv, device_id=to, device_id_type=MESH
        )

    def arrival(dst, send, recv):
        remote(dst, dst, send, recv, mate).wait_recv()

    load_a = pltpu.make_async_copy(fit_a, a_own, load_sem.at[0])
    load_b = pltpu.make_async_copy(fit_b.at[pl.ds(k * B_CORE, B_CORE)], b_own, load_sem.at[1])
    load_t = pltpu.make_async_copy(tiles, slots.at[me, pl.ds(0, rows_dev)], load_sem.at[2])
    load_o = pltpu.make_async_copy(owner, owners, load_sem.at[3])
    load_u = pltpu.make_async_copy(sub_block, subs, load_sem.at[4])
    for load in (load_o, load_u, load_t, load_a, load_b):
        load.start()

    barrier = pltpu.get_barrier_semaphore()

    across = device(x, y, far, k)
    for to in (mate, along(0), along(1), across):
        pl.semaphore_signal(barrier, inc=1, device_id=to, device_id_type=MESH)
    for i in range(1, PLANE):
        to = device(mod(x + i // RING), mod(y + i % RING), z, k)
        pl.semaphore_signal(barrier, inc=1, device_id=to, device_id_type=MESH)
    load_o.wait()
    load_u.wait()
    spot = (owners[...] * BLOCKS_OWNER + subs[...]) * 8 + lax.div(
        lax.broadcasted_iota(jnp.int32, owners.shape, 1), TILES_PAIR
    )
    slots[me, rows_dev : rows_dev + 16, :] = jnp.concatenate([spot, spot], axis=0).astype(F32).astype(BF16)
    row_ids[...] = lax.broadcasted_iota(jnp.int32, row_ids.shape, 0).astype(F32).astype(BF16)

    pl.semaphore_wait(barrier, PLANE + 3)

    def swap_a(i):
        rows = pl.ds(pl.multiple_of(mod(z + (2, 1, 3, 0)[i]) * ROWS, ROWS), ROWS)
        return remote(fit_a.at[rows], a_mate.at[rows], mate_s.at[i], mate_r.at[i], mate)

    def swap_b(i):
        first, count = ((0, 2), (2, 2), (4, 4))[i]
        here, there = pl.ds((1 - k) * B_CORE + first, count), pl.ds(first, count)
        return remote(fit_b.at[here], b_mate.at[there], mate_s.at[4 + i], mate_r.at[4 + i], mate)

    for swap in (swap_a(0), swap_b(0), swap_b(1), swap_a(1), swap_a(2), swap_b(2), swap_a(3)):
        swap.start()

    def ring1(g, d):
        ref = part_of(g, 0, 0)
        return remote(ref, ref, ring1_s.at[g, d], ring1_r.at[g, d], plane_device(g, 1 + 2 * d, 0))

    def half_ref(g, d, back):
        first = sizes[g] // 32 * 16
        return part_of(g, back, 0, d * first, sizes[g] - first if d else first)

    def half1(g, d):
        ref = half_ref(g, d, 3 - 2 * d)
        return remote(ref, ref, half1_s.at[g, d], half1_r.at[g, d], plane_device(g, 1 + 2 * d, 0))

    def ring2(g, d, i):
        ref = part_of(g, i, 0)
        return remote(ref, ref, ring2_s.at[g, d, i], ring2_r.at[g, d, i], plane_device(g, 0, 1 + 2 * d))

    def pass2(g, i):
        d = i // 2
        ref = part_of(g, i, 3 - 2 * d)
        return remote(ref, ref, pass2_s.at[g, i], pass2_r.at[g, i], plane_device(g, 0, 1 + 2 * d))

    def both_ways(i):
        for g in range(2):
            for d in (0, 1):
                ring2(g, d, i).start()

    def pass_on(d, i):
        for g in range(2):
            arrival(part_of(g, i, 3 - 2 * d), ring2_s.at[g, d, i], ring2_r.at[g, d, i])
            if i // 2 == d:
                pass2(g, i).start()

    load_t.wait()
    for g in range(2):
        for d in (0, 1):
            ring1(g, d).start()
    both_ways(0)
    load_a.wait()
    load_b.wait()

    def partial(part, h, t):
        rows = pl.ds(pl.multiple_of(part * ROWS, ROWS), ROWS)
        b = t * 4 + h * 2
        own = product(a_own[rows, :], jnp.concatenate([b_own[b], b_own[b + 1]], axis=1), 0)
        return own + product(a_mate[rows, :], jnp.concatenate([b_mate[b], b_mate[b + 1]], axis=1), 0)

    def far_copy(s, d):
        return remote(far_out.at[s, d], far_in.at[s, d], far_s.at[s, d], far_r.at[s, d], along(d))

    def side_copy(s, d):
        return remote(side_out.at[s, d], side_in.at[s, d], side_s.at[s, d], side_r.at[s, d], along(d))

    def comb_copy(s, d):
        return remote(comb_out.at[s, d], comb_in.at[s, d], comb_s.at[s, d], comb_r.at[s, d], along(d))

    def x_copy(s, i):
        rows = pl.ds(i * X_ROWS, X_ROWS)
        return remote(x_out.at[s, rows], x_in.at[s, rows], x_s.at[s, i], x_r.at[s, i], partner)

    def keep(ref, t, d, value):
        ref[2 * t, d] = value[:, :ND].astype(ref.dtype)
        ref[2 * t + 1, d] = value[:, ND:].astype(ref.dtype)

    def far_piece(t, d):
        keep(far_out, t, d, partial(far, d, t))

    def side_piece(t, d):
        keep(side_out, t, d, partial(mod(z + 1 + 2 * d), 1 - d, t))

    def comb_piece(t, d):
        keep(keep_comb, t, d, partial(mod(z + 1 + 2 * d), d, t))

    def own_piece(t, d):
        keep(keep_own, t, d, partial(z, d, t))

    def each_way(t, piece):
        def one(d, carry):
            piece(t, d)
            return carry

        lax.fori_loop(0, 2, one, 0)

    def both(s, copy):
        copy(s, 0).start()
        copy(s, 1).start()

    def send_comb(s):
        for d in (0, 1):
            far_copy(s, d).wait_recv()
            comb_out[s, d] = (keep_comb[s, d] + far_in[s, d].astype(F32)).astype(BF16)
            comb_copy(s, d).start()

    def build(slot):
        names[...] = slots[slot, pl.ds(rows_dev, 16), :].astype(F32)
        none = jnp.zeros((128, ND), BF16)

        def chosen(row):
            line = jnp.broadcast_to(names[row : row + 1, :], (16, 128)).astype(BF16)
            return jnp.where(row_ids[...] == jnp.concatenate([line] * 16, axis=0), 1.0, 0.0).astype(BF16)

        for j in range(rows_dev // STEP):
            choice = jnp.concatenate([chosen(2 * j), chosen(2 * j + 1)], axis=1)
            first = slots[slot, j * STEP : j * STEP + 128, :]
            second = slots[slot, j * STEP + 128 : (j + 1) * STEP, :]
            values = jnp.concatenate(
                [jnp.concatenate([first, none], axis=1), jnp.concatenate([none, second], axis=1)], axis=0
            )
            sums = product(choice, values, 0)
            rows = pl.ds(pl.multiple_of(slot * pairs_dev + j * 16, 16), 16)
            for c in range(NC):
                part = sums[c * 8 : (c + 1) * 8]
                part = jnp.concatenate([part[:, :ND], part[:, ND:]], axis=0)
                summed[c // 4, rows, (c % 4) * ND : (c % 4 + 1) * ND] = part.astype(BF16)

    def build_near(dx, first, last):
        def one(i, carry):
            build(mod(x + dx) * RING + mod(y + i + i // 2))
            return carry

        lax.fori_loop(first, last, one, 0)

    def build_far(first, last):
        def one(i, carry):
            build(mod(x + 2) * RING + mod(y + i))
            return carry

        lax.fori_loop(first, last, one, 0)

    def send_x(s):
        comb_copy(s, 0).wait_recv()
        comb_copy(s, 1).wait_recv()
        side_copy(s, 0).wait_recv()
        side_copy(s, 1).wait_recv()
        h = 1 - x_lo
        x_out[s] = (keep_own[s, h] + comb_in[s, h].astype(F32) + side_in[s, 1 - h].astype(F32)).astype(BF16)
        for i in range(X_PARTS):
            x_copy(s, i).start()

    def ag_copy(s, d):
        ref = ints.at[s, z, k]
        return remote(ref, ref, ag_s.at[s, d], ag_r.at[s, d], along(d))

    def fw_ref(s, part, core, d):
        return ints.at[s, part, core, :, pl.ds(d * STEP, STEP)]

    def fw_copy(s, d):
        ref = fw_ref(s, mod(z + 3 - 2 * d), k, d)
        return remote(ref, ref, fw_s.at[s, d], fw_r.at[s, d], along(d))

    def across_copy(s):
        ref = ints.at[s, z, k]
        return remote(ref, ref, fw_s.at[s, 0], fw_r.at[s, 0], across)

    def cx_ref(s, i, core):
        if i < 3:
            return ints.at[s, (z, down, up)[i], core]
        return fw_ref(s, far, core, i - 3)

    def cx_copy(s, i):
        ref = cx_ref(s, i, k)
        return remote(ref, ref, cx_s.at[s, i], cx_r.at[s, i], mate)

    def finish(s):
        for i in range(X_PARTS):
            x_copy(s, i).wait_recv()
        h = x_lo
        blocks = []
        for two in range(C_PART // 2):
            rows = pl.ds(two * 2 * NA, 2 * NA)
            value = (
                keep_own[s, h, rows, :]
                + comb_in[s, h, rows, :].astype(F32)
                + side_in[s, 1 - h, rows, :].astype(F32)
                + x_in[s, rows, :].astype(F32)
            )
            blocks += [value[:NA], value[NA:]]
        lines = [jnp.concatenate(blocks[i * 4 : i * 4 + 4], axis=1) for i in range(2)]
        ints[s, z, k] = jnp.concatenate(lines, axis=0).astype(BF16)
        ag_copy(s, 0).start()
        ag_copy(s, 1).start()
        cx_copy(s, 0).start()

    def forward(s):
        for d in (0, 1):
            from_z = mod(z + 3 - 2 * d)
            arrival(ints.at[s, from_z, k], ag_s.at[s, d], ag_r.at[s, d])
            if s < SLICES - 1:
                fw_copy(s, d).start()
            cx_copy(s, 1 + d).start()

    def last_forward(s):
        for d in (0, 1):
            if s < SLICES - 1:
                arrival(fw_ref(s, far, k, d), fw_s.at[s, d], fw_r.at[s, d])
            elif d == 0:
                arrival(ints.at[s, far, k], fw_s.at[s, 0], fw_r.at[s, 0])
            cx_copy(s, 3 + d).start()

    def multiply(t, parts, first):
        left = []
        for part in parts:
            values = [ints[s, part, core].astype(F32) for s in (2 * t, 2 * t + 1) for core in range(CORES)]
            left.append(jnp.concatenate([value[:NA] for value in values], axis=0).astype(BF16))
            left.append(jnp.concatenate([value[NA:] for value in values], axis=0).astype(BF16))

        def one(n, carry):
            rows = pl.ds(pl.multiple_of(n * 512, 512), 512)
            value = 0.0
            for at, part in enumerate(parts):
                for half in range(2):
                    value = value + product(summed[part * 2 + half, rows, :], left[2 * at + half], 1)
            total[t, rows, : 4 * NA] = value if first else total[t, rows, : 4 * NA] + value
            return carry

        lax.fori_loop(0, total.shape[1] // 512, one, 0)

    def gathered(t, *which):
        for i in which:
            for s in (2 * t, 2 * t + 1):
                arrival(cx_ref(s, i, 1 - k), cx_s.at[s, i], cx_r.at[s, i])
                if i == 3:
                    arrival(cx_ref(s, 4, 1 - k), cx_s.at[s, 4], cx_r.at[s, 4])
        multiply(t, [(z, down, up, far)[i] for i in which], 0 in which)

    def finish_out(t):
        gathered(t, 3)
        send_out(t)

    def out_copy(t, i):
        x_at, y_at = mod(x + i // RING), mod(y + i % RING)
        return remote(
            parcels.at[t, x_at * RING + y_at], got.at[t, me], out_s.at[t, i], out_r.at[t, i], device(x_at, y_at, z, k)
        )

    def send_out(t):
        low = lax.broadcasted_iota(jnp.int32, (OUT_ROWS, 128), 1) < 64
        for n in range(PLANE // 2):
            rows = slice(n * 128, (n + 1) * 128)
            value = jnp.concatenate([total[t, rows, :128].T, total[t, rows, 128:].T[: 4 * NA - 128]], axis=0)
            top = jnp.concatenate([value[i * NA : i * NA + A_HALF] for i in range(4)], axis=0)
            bottom = jnp.concatenate([value[i * NA + A_HALF : (i + 1) * NA] for i in range(4)], axis=0)
            parcels[t, 2 * n] = jnp.where(low, top, pltpu.roll(bottom, 64, 1)).astype(BF16)
            parcels[t, 2 * n + 1] = jnp.where(low, pltpu.roll(top, 64, 1), bottom).astype(BF16)
        for i in FARTHEST_FIRST[0] + FARTHEST_FIRST[1]:
            out_copy(t, i).start()

    def unpack(t, x_at, y_at, value):
        base = (lax.div(x_at, 2) * RING + y_at) * 16 + t * 4 + lax.rem(x_at, 2) * 2
        for at in range(4):
            rows = pl.ds(pl.multiple_of((base + at % 2 * 8 + at // 2) * B_STRIDE, 8), A_HALF)
            final[rows, :] = value[at * A_HALF : (at + 1) * A_HALF]

    def receive(t):
        unpack(t, x, y, parcels[t, me].astype(F32))

        for i in FARTHEST_FIRST[0] + FARTHEST_FIRST[1]:
            x_at, y_at = mod(x + RING - i // RING), mod(y + RING - i % RING)
            slot = x_at * RING + y_at
            arrival(got.at[t, slot], out_s.at[t, i], out_r.at[t, i])
            unpack(t, x_at, y_at, got[t, slot].astype(F32))

    swap_a(0).wait_recv()
    for d in (0, 1):
        swap_b(d).wait_recv()
        far_piece(0, d)
        far_copy(0, d).start()
        far_copy(1, d).start()
    swap_a(1).wait_recv()
    swap_a(2).wait_recv()
    each_way(0, side_piece)
    both(0, side_copy)
    each_way(0, comb_piece)
    for g in range(2):
        for d in (0, 1):
            arrival(part_of(g, 3 - 2 * d, 0), ring1_s.at[g, d], ring1_r.at[g, d])
            half1(g, d).start()
    both_ways(3)
    both_ways(1)
    swap_b(2).wait_recv()
    swap_a(3).wait_recv()
    each_way(1, far_piece)
    send_comb(0)
    both(1, side_copy)
    send_comb(1)
    both(2, far_copy)
    both(3, far_copy)
    for g in range(2):
        for d in (0, 1):
            arrival(half_ref(g, d, 2), half1_s.at[g, d], half1_r.at[g, d])
    both_ways(2)
    each_way(1, side_piece)
    both(2, side_copy)
    each_way(1, comb_piece)
    each_way(0, own_piece)
    each_way(1, own_piece)
    send_x(0)
    pass_on(0, 0)
    pass_on(1, 3)
    build_near(0, 0, 1)
    send_x(1)
    pass_on(0, 1)
    send_comb(2)
    both(3, side_copy)
    pass_on(1, 2)
    for d, i in ((0, 3), (0, 2), (1, 0), (1, 1)):
        pass_on(d, i)
    send_comb(3)
    build_near(0, 1, 3)
    finish(0)
    build_near(1, 0, 3)
    finish(1)
    send_x(2)
    build_near(3, 0, 3)
    send_x(3)
    finish(2)
    for g in range(2):
        for i in range(RING):
            arrival(part_of(g, i, 2), pass2_s.at[g, i], pass2_r.at[g, i])
    build_far(0, RING)
    forward(0)
    for dx in (0, 1, 3):
        build(mod(x + dx) * RING + mod(y + 2))
    forward(1)
    finish(3)
    gathered(0, 0)
    forward(2)
    across_copy(SLICES - 1).start()
    gathered(0, 1, 2)
    last_forward(0)
    last_forward(1)
    gathered(1, 0)
    forward(3)
    finish_out(0)
    last_forward(2)
    last_forward(3)
    gathered(1, 1, 2)
    finish_out(1)
    for t in range(GROUPS):
        receive(t)
    for i in range(A_HALF):
        value = final[pl.ds(i, NB, stride=B_STRIDE), :]
        turned = value.T.astype(BF16)
        out[:, i * NB : (i + 1) * NB] = turned[:pairs_dev]
        out[:, (i + A_HALF) * NB : (i + A_HALF + 1) * NB] = turned[pairs_dev:]

    for i in range(RING):
        swap_a(i).wait_send()
    for i in range(3):
        swap_b(i).wait_send()
    for g in range(2):
        for d in (0, 1):
            ring1(g, d).wait_send()
            half1(g, d).wait_send()
            for i in range(RING):
                ring2(g, d, i).wait_send()
        for i in range(RING):
            pass2(g, i).wait_send()
    for s in range(SLICES):
        for i in range(X_PARTS):
            x_copy(s, i).wait_send()
        for d in (0, 1):
            far_copy(s, d).wait_send()
            side_copy(s, d).wait_send()
            comb_copy(s, d).wait_send()
            ag_copy(s, d).wait_send()
            if s < SLICES - 1:
                fw_copy(s, d).wait_send()
            elif d == 0:
                across_copy(s).wait_send()
        for i in range(5):
            cx_copy(s, i).wait_send()

    for t in range(GROUPS):
        for i in FARTHEST_FIRST[0] + FARTHEST_FIRST[1]:
            out_copy(t, i).wait_send()


def on_device(tiles, owner, sub_block, fit_ac, fit_bd):
    rows_dev = tiles.shape[0]
    depth = fit_ac.shape[2]
    owner = owner.reshape(rows_dev // 128, 128)
    sub_block = sub_block.reshape(rows_dev // 128, 128)
    fit_a = fit_ac.reshape(NC * NA, depth)
    fit_b = jnp.swapaxes(fit_bd, 1, 2)
    pairs = rows_dev // TILES_PAIR * PLANE
    dma = pltpu.SemaphoreType.DMA
    return pl.pallas_call(
        kernel,
        out_shape=pltpu.VMEM((rows_dev // TILES_PAIR, NA * NB), BF16),
        in_specs=[pl.BlockSpec(memory_space=pl.ANY)] * 5,
        out_specs=pl.BlockSpec(memory_space=pltpu.VMEM),
        scratch_shapes=[
            pltpu.VMEM((NC * NA, depth), BF16),
            pltpu.VMEM((NC * NA, depth), BF16),
            pltpu.VMEM((B_CORE, depth, ND), BF16),
            pltpu.VMEM((B_CORE, depth, ND), BF16),
            pltpu.VMEM((PLANE, rows_dev + 16, ND), BF16),
            *[pltpu.VMEM((SLICES, 2, ROWS, ND), BF16)] * 6,
            *[pltpu.VMEM((SLICES, 2, ROWS, ND), F32)] * 2,
            *[pltpu.VMEM((SLICES, ROWS, ND), BF16)] * 2,
            pltpu.VMEM((SLICES, RING, CORES, 2 * NA, K_HALF), BF16),
            pltpu.VMEM((2 * RING, pairs, K_HALF), BF16),
            pltpu.VMEM((GROUPS, pairs, STEP), F32),
            *[pltpu.VMEM((GROUPS, PLANE, OUT_ROWS, 128), BF16)] * 2,
            *[pltpu.VMEM((rows_dev // 128, 128), jnp.int32)] * 2,
            pltpu.VMEM((STEP, 128), BF16),
            pltpu.VMEM((16, 128), F32),
            pltpu.VMEM(((NB + 1) * B_STRIDE, 128), F32),
            dma((5,)),
            dma((7,)), dma((7,)),
            *[dma((2, 2))] * 4,
            *[dma((2, 2, RING))] * 2,
            *[dma((2, RING))] * 2,
            *[dma((SLICES, 2))] * 6,
            *[dma((SLICES, X_PARTS))] * 2,
            *[dma((SLICES, 2))] * 4,
            *[dma((SLICES, 5))] * 2,
            *[dma((GROUPS, PLANE))] * 2,
        ],
        compiler_params=pltpu.CompilerParams(
            collective_id=0, has_side_effects=True, vmem_limit_bytes=56 * 1024 * 1024
        ),
        cost_estimate=pl.CostEstimate(flops=7 * 10**9, bytes_accessed=4 * 10**6, transcendentals=0),
        name="ladder",
    )(tiles, owner, sub_block, fit_a, fit_b)


def solution(mesh):
    placed = (
        P(("blk", "occ"), None),
        P(("blk", "occ"), None),
        P(("blk", "occ")),
        P(None, None, "occ"),
        P("blk", None, "occ"),
    )
    return jax.shard_map(
        on_device, mesh=mesh, in_specs=placed, out_specs=P(("blk", "occ"), None), check_vma=False
    )
```

profile of v0, /device:TPU:1, one launch (start us, length us, event | category | flops | bytes accessed | tf_op | source)
XLA Modules:
  0.0 58.2 jit_solution(1290721220953281939)
XLA Ops:
  0.0 57.3 %ladder.1 = bf16[64,5120]{1,0:T(8,128)(2,1)S(1)} custom-call(bf16[1024,128]{1,0:T(8,128)(2,1)} %tiles.1, s32[8,128]{1,0:T(8,128)} %bitcast.6, s32[8,128]{1,0:T(8,128)} %bitcast.7, bf16[1280,400]{1,0:T(8,128)(2,1)} %bitcast.5, bf16[16,400,128]{2,1,0:T(8,128)(2,1)} %bitcast.4), custom_call_target="tpu_custom_call" | custom-call | flops 7000000000 | bytes 4000000 | tf_op jit(solution)/shard_map/ladder/pallas_call | solution.py:511
  57.3 0.8 %copy.7 = bf16[64,5120]{1,0:T(8,128)(2,1)} copy(bf16[64,5120]{1,0:T(8,128)(2,1)S(1)} %ladder.1) | data formatting | bytes 1310720
where the time goes:
time: 58.3 us; the launch traced here: 58.2 us
  Pallas kernels  57.3 us (98%)
  local copies, waits for them, and re-layouts  0.84 us (1%)
    pallas_call x1, Pallas kernels, on_device(): pl.pallas_call(kernel, out_shape=pltpu.VMEM((rows_dev // TILES_PAIR, NA *...  57.3 us

commit v1 on v0

--- a/solution.py
+++ b/solution.py
@@ -37,7 +37,7 @@
 def kernel(
     tiles, owner, sub_block, fit_a, fit_b, out,
     a_own, a_mate, b_own, b_mate, slots, far_out, side_out, comb_out, far_in, side_in, comb_in,
-    keep_comb, keep_own, x_out, x_in, ints, summed, total, parcels, got, owners, subs, row_ids, names, final,
+    keep_comb, keep_own, x_out, x_in, ints, summed, total, parcels, got, owners, subs, row_ids, names, final, begun,
     load_sem, mate_s, mate_r, ring1_s, ring1_r, half1_s, half1_r, ring2_s, ring2_r, pass2_s, pass2_r,
     far_s, far_r, side_s, side_r, comb_s, comb_r, x_s, x_r, ag_s, ag_r, fw_s, fw_r, cx_s, cx_r, out_s, out_r,
 ):
@@ -108,6 +108,22 @@
     slots[me, rows_dev : rows_dev + 16, :] = jnp.concatenate([spot, spot], axis=0).astype(F32).astype(BF16)
     row_ids[...] = lax.broadcasted_iota(jnp.int32, row_ids.shape, 0).astype(F32).astype(BF16)
 
+    load_a.wait()
+    load_b.wait()
+
+    def share(left, right, part, h, t):
+        rows = pl.ds(pl.multiple_of(part * ROWS, ROWS), ROWS)
+        b = t * 4 + h * 2
+        return product(left[rows, :], jnp.concatenate([right[b], right[b + 1]], axis=1), 0)
+
+    def partial(part, h, t):
+        return share(a_own, b_own, part, h, t) + share(a_mate, b_mate, part, h, t)
+
+    def begin(d, carry):
+        begun[d] = share(a_own, b_own, far, d, 0)
+        return carry
+
+    lax.fori_loop(0, 2, begin, 0)
     pl.semaphore_wait(barrier, PLANE + 3)
 
     def swap_a(i):
@@ -159,14 +175,6 @@
         for d in (0, 1):
             ring1(g, d).start()
     both_ways(0)
-    load_a.wait()
-    load_b.wait()
-
-    def partial(part, h, t):
-        rows = pl.ds(pl.multiple_of(part * ROWS, ROWS), ROWS)
-        b = t * 4 + h * 2
-        own = product(a_own[rows, :], jnp.concatenate([b_own[b], b_own[b + 1]], axis=1), 0)
-        return own + product(a_mate[rows, :], jnp.concatenate([b_mate[b], b_mate[b + 1]], axis=1), 0)
 
     def far_copy(s, d):
         return remote(far_out.at[s, d], far_in.at[s, d], far_s.at[s, d], far_r.at[s, d], along(d))
@@ -386,7 +394,7 @@
     swap_a(0).wait_recv()
     for d in (0, 1):
         swap_b(d).wait_recv()
-        far_piece(0, d)
+        keep(far_out, 0, d, begun[d] + share(a_mate, b_mate, far, d, 0))
         far_copy(0, d).start()
         far_copy(1, d).start()
     swap_a(1).wait_recv()
@@ -530,6 +538,7 @@
             pltpu.VMEM((STEP, 128), BF16),
             pltpu.VMEM((16, 128), F32),
             pltpu.VMEM(((NB + 1) * B_STRIDE, 128), F32),
+            pltpu.VMEM((2, ROWS, 2 * ND), F32),
             dma((5,)),
             dma((7,)), dma((7,)),
             *[dma((2, 2))] * 4,

time: 58.3 us -> 58.2 us (level)
  no operation moved by 1% of the time
where the time goes in v1:
time: 58.2 us; the launch traced here: 58.1 us
  Pallas kernels  57.2 us (98%)
  local copies, waits for them, and re-layouts  0.84 us (1%)
    pallas_call x1, Pallas kernels, on_device(): pl.pallas_call(kernel, out_shape=pltpu.VMEM((rows_dev // TILES_PAIR, NA *...  57.2 us

profile of v1, /device:TPU:1, one launch (start us, length us, event | category | flops | bytes accessed | tf_op | source)
XLA Modules:
  0.0 58.1 jit_solution(15222876801122633998)
XLA Ops:
  0.0 57.2 %ladder.1 = bf16[64,5120]{1,0:T(8,128)(2,1)S(1)} custom-call(bf16[1024,128]{1,0:T(8,128)(2,1)} %tiles.1, s32[8,128]{1,0:T(8,128)} %bitcast.6, s32[8,128]{1,0:T(8,128)} %bitcast.7, bf16[1280,400]{1,0:T(8,128)(2,1)} %bitcast.5, bf16[16,400,128]{2,1,0:T(8,128)(2,1)} %bitcast.4), custom_call_target="tpu_custom_call" | custom-call | flops 7000000000 | bytes 4000000 | tf_op jit(solution)/shard_map/ladder/pallas_call | solution.py:519
  57.2 0.8 %copy.7 = bf16[64,5120]{1,0:T(8,128)(2,1)} copy(bf16[64,5120]{1,0:T(8,128)(2,1)S(1)} %ladder.1) | data formatting | bytes 1310720
